TPU v7x, 256 devices: a whole 4x4x8 slice. The times are simulated.
256 devices in a mesh: wide: 64 (over x, z, core), narrow: 4 (over y).
Axes of the slice: x: 4, y: 4, z: 8, core: 2. Of those that a mesh axis runs over, the one named last changes fastest.
Arguments:
- potentials: float32 [64, 128, 128, 128], P('wide', 'narrow'), may hold values from -190 to 190
- parents: int32 [64], replicated, may hold values from 0 to 20, as said below
- separator_excluded: int32 [64], replicated, may hold values from 0 to 2
- measurement_clique: int32 [64], replicated, may hold values from 0 to 63, as said below
- measured: float32 [64, 128, 128], P('wide', 'narrow'), may hold values from 0.25 to 4
Outputs:
- marginal: float32 [64, 128, 128], P('wide', 'narrow')
- updated: float32 [64, 128, 128, 128], P('wide', 'narrow')
Inputs may be any that keep to these rules, and one draw needn't show every extreme that they name: parents[0] = 0; a clique c with 1 <= c < 5 has parent 0, one with 5 <= c < 21 a parent in 1 to 4, and one with c >= 21 a parent in 5 to 20; the last clique has parent 21 - 1. `measurement_clique`: every clique is named by exactly one measured marginal.
All inputs are finite; a program needn't handle non-finite values.
Results may differ from a plain program's by a relative error of at most 0.0003.
Values sent between devices are 32-bit elements; how exact they have to be, the bound alone decides.
A program may use at most 64 MiB of HBM per device.

v0:
```python
import jax
import jax.numpy as jnp
from jax import lax
from jax.sharding import PartitionSpec as P

DEPTH = 3


def merged_2(part, axis, combine):
    gathered = jax.tree.map(lambda a: lax.all_gather(a, axis), part)

    def take(source):
        return jax.tree.map(lambda a: lax.dynamic_index_in_dim(a, source, 0, False), gathered)

    return lax.fori_loop(
        1, lax.axis_size(axis), lambda source, state: combine(state, take(source)), take(0)
    )


def log_sum(values, along):
    largest_entry = jnp.max(values, axis=along, keepdims=True)
    return jnp.squeeze(largest_entry, along) + jnp.log(
        jnp.sum(jnp.exp(values - largest_entry), axis=along)
    )


def join_tables(first, second):
    largest_entry = jnp.maximum(first[0], second[0])
    return (
        largest_entry,
        first[1] * jnp.exp(first[0] - largest_entry)
        + second[1] * jnp.exp(second[0] - largest_entry),
    )


def outgoing(belief, quarter_index, rows_here):
    largest_entry = jnp.max(belief, axis=0)
    summed = jnp.sum(jnp.exp(belief - largest_entry[None]), axis=0)
    merged = merged_2((largest_entry, summed), "narrow", join_tables)
    drop_first = merged[0] + jnp.log(merged[1])
    drop_first = lax.dynamic_slice_in_dim(drop_first, quarter_index * rows_here, rows_here, 0)
    return jnp.stack([drop_first, log_sum(belief, 1), log_sum(belief, 2)])


def body(potentials, parents, separator_excluded, measurement_clique, measured):
    own_slab = potentials[0]
    rows_here = own_slab.shape[0]
    domain = own_slab.shape[2]
    wide_count = lax.axis_size("wide")
    self_index = lax.axis_index("wide")
    quarter_index = lax.axis_index("narrow")
    first_leaf = 1 + max(1, wide_count // 16) + wide_count // 4
    parent_row = parents[self_index]
    kind_row = separator_excluded[self_index]
    belief = own_slab
    for iteration in range(DEPTH):
        tables = outgoing(belief, quarter_index, rows_here)
        gathered = lax.all_gather(tables[None], "wide", axis=0, tiled=True)
        picked = gathered[parent_row, kind_row]
        complete = lax.all_gather(picked, "narrow", axis=0, tiled=True)
        complete = jnp.where(self_index > 0, complete, jnp.float32(0.0))
        belief = own_slab + complete[None]
    scale = jnp.float32(domain * domain)
    largest_entry = jnp.max(belief)
    summed = jnp.sum(jnp.exp(belief - largest_entry))
    merged = merged_2((largest_entry, summed), "narrow", join_tables)
    logz = merged[0] + jnp.log(merged[1])
    weighted = scale * jnp.sum(jnp.exp(belief - logz), axis=0)
    marginal = lax.psum_scatter(weighted, "narrow", scatter_dimension=0, tiled=True)
    source_row = jnp.sum(
        jnp.where(
            measurement_clique == self_index,
            jnp.arange(measurement_clique.shape[0], dtype=jnp.int32),
            0,
        )
    )
    pieces = lax.all_gather(measured, "wide", axis=0, tiled=True)
    row_ids = jnp.arange(pieces.shape[0], dtype=jnp.int32)
    selector = (row_ids == source_row).astype(jnp.float32)
    own_measure = jnp.einsum("m,mqk->qk", selector, pieces, precision=lax.Precision.HIGHEST)
    residual = marginal - own_measure
    residual_whole = lax.all_gather(residual, "narrow", axis=0, tiled=True)
    step_term = jnp.where(self_index >= first_leaf, residual_whole, jnp.float32(0.0))
    updated = own_slab - jnp.float32(0.5) * step_term[None]
    return (marginal[None], updated[None])


def solution(mesh):
    return jax.shard_map(
        body,
        mesh=mesh,
        in_specs=(P("wide", "narrow", None, None), P(), P(), P(), P("wide", "narrow", None)),
        out_specs=(P("wide", "narrow", None), P("wide", "narrow", None, None)),
        check_vma=False,
    )
```

profile of v0, /device:TPU:2, one launch (start us, length us, event | category | flops | bytes accessed | tf_op | source)
XLA Modules:
  0.0 470.5 jit_solution(12748854386773682030)
XLA Ops:
  7.2 2.4 fusion.29
  9.6 12.8 %all-gather = f32[512,128]{1,0:T(8,128)S(1)} all-gather(f32[128,128]{1,0:T(8,128)S(1)} %get-tuple-element.555), channel_id=2, replica_groups=mesh['wide'=64,'narrow'=4] {'narrow'}, dimensions={0}, use_global_device_ids=true | all-gather | bytes 327680 | tf_op jit(solution)/shard_map/all_gather | solution.py:10
  22.4 1.5 fusion.7
  23.9 12.3 %all-gather.1 = f32[512,128]{1,0:T(8,128)S(1)} all-gather(f32[128,128]{1,0:T(8,128)S(1)} %get-tuple-element.552), channel_id=3, replica_groups=mesh['wide'=64,'narrow'=4] {'narrow'}, dimensions={0}, use_global_device_ids=true | all-gather | bytes 327680 | tf_op jit(solution)/shard_map/all_gather | solution.py:10
  42.2 74.5 %all-gather.19.cloned.1.call-done = f32[192,32,128]{2,1,0:T(8,128)} async-done(((f32[3,32,128]{2,1,0:T(8,128)}), f32[192,32,128]{2,1,0:T(8,128)}) %all-gather.19.cloned.1.call-update) | async-done | bytes 3145744 | tf_op jit(solution)/shard_map/all_gather | solution.py:58
  116.7 0.7 constant_dynamic-slice_fusion.2
  117.4 12.2 %all-gather.3 = f32[1,1,128,128]{3,2,1,0:T(8,128)S(1)} all-gather(f32[1,1,32,128]{3,2,1,0:T(8,128)S(1)} %constant_dynamic-slice_fusion.2), channel_id=5, replica_groups=mesh['wide'=64,'narrow'=4] {'narrow'}, dimensions={2}, use_global_device_ids=true | all-gather | bytes 81920 | tf_op jit(solution)/shard_map/all_gather | solution.py:60
  130.4 12.3 %all-gather.4 = f32[512,128]{1,0:T(8,128)S(1)} all-gather(f32[128,128]{1,0:T(8,128)S(1)} %fusion.15), channel_id=6, replica_groups=mesh['wide'=64,'narrow'=4] {'narrow'}, dimensions={0}, use_global_device_ids=true | all-gather | bytes 327680 | tf_op jit(solution)/shard_map/all_gather | solution.py:10
  142.7 12.2 %all-gather.5 = f32[512,128]{1,0:T(8,128)S(1)} all-gather(f32[128,128]{1,0:T(8,128)S(1)} %get-tuple-element.547), channel_id=7, replica_groups=mesh['wide'=64,'narrow'=4] {'narrow'}, dimensions={0}, use_global_device_ids=true | all-gather | bytes 327680 | tf_op jit(solution)/shard_map/all_gather | solution.py:10
  155.2 1.3 exponential_reduce_fusion.6
  157.3 75.3 %all-gather.21.cloned.1.call-done = f32[192,32,128]{2,1,0:T(8,128)} async-done(((f32[3,32,128]{2,1,0:T(8,128)}), f32[192,32,128]{2,1,0:T(8,128)}) %all-gather.21.cloned.1.call-update) | async-done | bytes 3145744 | tf_op jit(solution)/shard_map/all_gather | solution.py:58
  232.6 0.7 constant_dynamic-slice_fusion.1
  233.3 12.2 %all-gather.7 = f32[1,1,128,128]{3,2,1,0:T(8,128)S(1)} all-gather(f32[1,1,32,128]{3,2,1,0:T(8,128)S(1)} %constant_dynamic-slice_fusion.1), channel_id=9, replica_groups=mesh['wide'=64,'narrow'=4] {'narrow'}, dimensions={2}, use_global_device_ids=true | all-gather | bytes 81920 | tf_op jit(solution)/shard_map/all_gather | solution.py:60
  246.4 12.3 %all-gather.8 = f32[512,128]{1,0:T(8,128)S(1)} all-gather(f32[128,128]{1,0:T(8,128)S(1)} %fusion.18), channel_id=10, replica_groups=mesh['wide'=64,'narrow'=4] {'narrow'}, dimensions={0}, use_global_device_ids=true | all-gather | bytes 327680 | tf_op jit(solution)/shard_map/all_gather | solution.py:10
  258.6 12.2 %all-gather.9 = f32[512,128]{1,0:T(8,128)S(1)} all-gather(f32[128,128]{1,0:T(8,128)S(1)} %get-tuple-element.542), channel_id=11, replica_groups=mesh['wide'=64,'narrow'=4] {'narrow'}, dimensions={0}, use_global_device_ids=true | all-gather | bytes 327680 | tf_op jit(solution)/shard_map/all_gather | solution.py:10
  271.2 1.3 exponential_reduce_fusion.3
  274.5 0.6 fusion.26
  275.1 73.4 %all-gather.23.cloned.1.call-done = f32[192,32,128]{2,1,0:T(8,128)} async-done(((f32[3,32,128]{2,1,0:T(8,128)}), f32[192,32,128]{2,1,0:T(8,128)}) %all-gather.23.cloned.1.call-update) | async-done | bytes 3145744 | tf_op jit(solution)/shard_map/all_gather | solution.py:58
  348.6 0.7 constant_dynamic-slice_fusion
  349.3 12.2 %all-gather.11 = f32[1,1,128,128]{3,2,1,0:T(8,128)S(1)} all-gather(f32[1,1,32,128]{3,2,1,0:T(8,128)S(1)} %constant_dynamic-slice_fusion), channel_id=13, replica_groups=mesh['wide'=64,'narrow'=4] {'narrow'}, dimensions={2}, use_global_device_ids=true | all-gather | bytes 81920 | tf_op jit(solution)/shard_map/all_gather | solution.py:60
  361.5 1.2 fusion.12
  362.6 1.9 exponential_reduce_fusion.1
  364.5 1.4 dynamic-update-slice.1
  365.9 1.4 dynamic-update-slice
  367.3 10.1 %all-reduce.2 = (f32[4]{0:T(128)S(1)}, f32[4]{0:T(128)S(1)}) all-reduce(f32[4]{0:T(128)S(1)} %dynamic-update-slice, f32[4]{0:T(128)S(1)} %dynamic-update-slice.1), channel_id=1, replica_groups=mesh['wide'=64,'narrow'=4] {'narrow'}, use_global_device_ids=true, to_apply=%add | all-reduce | flops 8 | bytes 64
  377.5 9.7 %while.71 = (s32[]{:T(128)}, f32[]{:T(128)}, f32[]{:T(128)}, f32[4]{0:T(128)S(1)}, f32[4]{0:T(128)S(1)}, /*index=5*/s32[]{:T(128)}, s32[]{:T(128)}, s32[]{:T(128)}) while((s32[]{:T(128)}, f32[]{:T(128)}, f32[]{:T(128)}, f32[4]{0:T(128)S(1)}, f32[4]{0:T(128)S(1)}, /*index=5*/s32[]{:T(128)}, s32[]{:T(128)}, s32[]{:T(128)}) %tuple.162), condition=%wide.region_27.28_spmd, body=%wide.region_26.27_spmd.sunk | while | flops 11 | bytes 247 | solution.py:15
  388.3 37.1 %all-gather.17.cloned.1.call-done = f32[64,32,128]{2,1,0:T(8,128)} async-done(((f32[1,32,128]{2,1,0:T(8,128)}), f32[64,32,128]{2,1,0:T(8,128)}) %all-gather.17.cloned.1.call-update) | async-done | bytes 1048592 | tf_op jit(solution)/shard_map/all_gather | solution.py:77
  425.3 2.8 fusion.19
  428.2 21.6 %reduce-scatter.2.cloned.1.call-done = f32[32,128]{1,0:T(8,128)} async-done(((f32[128,128]{1,0:T(8,128)}), f32[32,128]{1,0:T(8,128)}) %reduce-scatter.2.cloned.1.call-update) | async-done | bytes 16400 | tf_op jit(solution)/shard_map/reduce_scatter | solution.py:69
  449.8 0.7 sub.198
  450.5 11.9 %all_gather.95 = f32[128,128]{1,0:T(8,128)S(1)} all-gather(f32[32,128]{1,0:T(8,128)S(1)} %sub.198), channel_id=1, replica_groups=mesh['wide'=64,'narrow'=4] {'narrow'}, dimensions={0}, use_global_device_ids=true | all-gather | bytes 81920 | tf_op jit(solution)/shard_map/all_gather | solution.py:82
  462.4 1.6 broadcast_subtract_fusion
  (70 shorter events, 12.2 us)
Async XLA Ops:
  7.2 15.2 %copy-start = (f32[1,32,128,128]{3,2,1,0:T(8,128)S(1)}, f32[1,32,128,128]{3,2,1,0:T(8,128)}, u32[]{:S(2)}) copy-start(f32[1,32,128,128]{3,2,1,0:T(8,128)} %param.13) | copy-start | bytes 6291460
  7.2 109.5 %all-gather.19.cloned.1.call-start = ((), (), s32[]{:S(2)}) async-start(), calls=%async_computation.3 | async-start | bytes 3194880 | tf_op jit(solution)/shard_map/all_gather | solution.py:58
  23.9 13.3 %copy-start.1 = (s32[64]{0:T(128)S(1)}, s32[64]{0:T(128)}, u32[]{:S(2)}) copy-start(s32[64]{0:T(128)} %param.14) | copy-start | bytes 772
  23.9 15.2 %copy-start.2 = (s32[64]{0:T(128)S(1)}, s32[64]{0:T(128)}, u32[]{:S(2)}) copy-start(s32[64]{0:T(128)} %param.15) | copy-start | bytes 772
  37.1 195.5 %all-gather.21.cloned.1.call-start = ((), (), s32[]{:S(2)}) async-start(), calls=%async_computation.4 | async-start | bytes 3194880 | tf_op jit(solution)/shard_map/all_gather | solution.py:58
  157.3 191.3 %all-gather.23.cloned.1.call-start = ((), (), s32[]{:S(2)}) async-start(), calls=%async_computation.5 | async-start | bytes 3194880 | tf_op jit(solution)/shard_map/all_gather | solution.py:58
  270.9 3.0 copy-start.4
  270.9 3.6 copy-start.3
  273.2 152.1 %all-gather.17.cloned.1.call-start = ((), (), s32[]{:S(2)}) async-start(), calls=%async_computation.2 | async-start | bytes 1064960 | tf_op jit(solution)/shard_map/all_gather | solution.py:77
  273.8 176.0 %reduce-scatter.2.cloned.1.call-start = ((), (), s32[]{:S(2)}) async-start(), calls=%async_computation.1 | async-start | bytes 81920 | tf_op jit(solution)/shard_map/reduce_scatter | solution.py:69
Sparse Core Ops, SparseCore 0:
  37.3 79.3 all-gather.18
  157.4 75.1 all-gather.20
  273.3 75.1 all-gather.22
  351.2 74.1 all-gather.16
  428.2 21.4 reduce-scatter.1
where the time goes:
time: 471 us; the launch traced here: 470 us
  waiting for transfers between devices  282 us (60%)
  blocking collectives  133 us (28%)
  between operations  18 us (4%)
  other arithmetic  17.7 us (4%)
  local copies, waits for them, and re-layouts  10.3 us (2%)
  loops' own time  6.39 us (1%)
    all_gather x3, waiting for transfers between devices, body(): gathered = lax.all_gather(tables[None], 'wide', axis=0, tiled=True)  223 us
    all_gather x6, blocking collectives, merged_2(): gathered = jax.tree.map(lambda a: lax.all_gather(a, axis), part)  74.1 us
    all_gather x1, waiting for transfers between devices, body(): pieces = lax.all_gather(measured, 'wide', axis=0, tiled=True)  37.1 us
    all_gather x3, blocking collectives, body(): complete = lax.all_gather(picked, 'narrow', axis=0, tiled=True)  36.6 us
    reduce_scatter x1, waiting for transfers between devices, body(): lax.psum_scatter(weighted, 'narrow', scatter_dimension=0, tiled=True)  21.6 us
    all_gather x1, blocking collectives, body(): residual_whole = lax.all_gather(residual, 'narrow', axis=0, tiled=True)  11.9 us
    unnamed x1, blocking collectives  10.1 us
  transfers between devices with their start and end apart: 5, of which 5 were waited for; matrix products, arithmetic and copies ran while one was open for 3% of the time, Pallas kernels for 0%

commit v1 on v0

--- a/solution.py
+++ b/solution.py
@@ -57,7 +57,16 @@
         tables = outgoing(belief, quarter_index, rows_here)
         gathered = lax.all_gather(tables[None], "wide", axis=0, tiled=True)
         picked = gathered[parent_row, kind_row]
-        complete = lax.all_gather(picked, "narrow", axis=0, tiled=True)
+        ring = [picked]
+        for hop in range(3):
+            ring.append(
+                lax.ppermute(ring[-1], "narrow", [(dev, (dev + 1) % 4) for dev in range(4)])
+            )
+        complete = jnp.roll(
+            jnp.concatenate(ring[::-1], axis=0),
+            (lax.axis_index("narrow") + 1) * ring[0].shape[0],
+            axis=0,
+        )
         complete = jnp.where(self_index > 0, complete, jnp.float32(0.0))
         belief = own_slab + complete[None]
     scale = jnp.float32(domain * domain)

time: 471 us -> 475 us (level)
  blocking collectives: 133 us -> 93.8 us
  waiting for transfers between devices: 282 us -> 320 us
  starting transfers between devices: 0.2 us -> 5.49 us
    ppermute x0 -> x9, waiting for transfers between devices: none -> 38 us  [body(): lax.ppermute(ring[-1], 'narrow', [(dev, (dev + 1) % 4) for dev in range(4)])]
    all_gather x3 -> x0, blocking collectives: 36.6 us -> none  [body(): complete = lax.all_gather(picked, 'narrow', axis=0, tiled=True)]
    ppermute x0 -> x9, starting transfers between devices: none -> 5.29 us  [body(): lax.ppermute(ring[-1], 'narrow', [(dev, (dev + 1) % 4) for dev in range(4)])]
  transfers between devices with their start and end apart: 5 -> 14, of which waited for: 5 -> 14; matrix products, arithmetic and copies ran while one was open for 3% -> 3% of each run, Pallas kernels for 0% -> 0%
where the time goes in v1:
time: 475 us; the launch traced here: 474 us
  waiting for transfers between devices  320 us (67%)
  blocking collectives  93.8 us (20%)
  other arithmetic  18.2 us (4%)
  between operations  17.7 us (4%)
  local copies, waits for them, and re-layouts  10.1 us (2%)
  loops' own time  6.39 us (1%)
  starting transfers between devices  5.49 us (1%)
    all_gather x3, waiting for transfers between devices, body(): gathered = lax.all_gather(tables[None], 'wide', axis=0, tiled=True)  223 us
    all_gather x6, blocking collectives, merged_2(): gathered = jax.tree.map(lambda a: lax.all_gather(a, axis), part)  74.3 us
    ppermute x9, waiting for transfers between devices, body(): lax.ppermute(ring[-1], 'narrow', [(dev, (dev + 1) % 4) for dev in range(4)])  38 us
    all_gather x1, waiting for transfers between devices, body(): pieces = lax.all_gather(measured, 'wide', axis=0, tiled=True)  36.8 us
    reduce_scatter x1, waiting for transfers between devices, body(): lax.psum_scatter(weighted, 'narrow', scatter_dimension=0, tiled=True)  21.6 us
    all_gather x1, blocking collectives, body(): residual_whole = lax.all_gather(residual, 'narrow', axis=0, tiled=True)  11.9 us
  transfers between devices with their start and end apart: 14, of which 14 were waited for; matrix products, arithmetic and copies ran while one was open for 3% of the time, Pallas kernels for 0%

profile of v1, /device:TPU:2, one launch (start us, length us, event | category | flops | bytes accessed | tf_op | source)
XLA Modules:
  0.0 474.3 jit_solution(2533607886468477523)
XLA Ops:
  7.2 2.4 fusion.53
  9.6 12.8 %all-gather = f32[512,128]{1,0:T(8,128)S(1)} all-gather(f32[128,128]{1,0:T(8,128)S(1)} %get-tuple-element.556), channel_id=2, replica_groups=mesh['wide'=64,'narrow'=4] {'narrow'}, dimensions={0}, use_global_device_ids=true | all-gather | bytes 327680 | tf_op jit(solution)/shard_map/all_gather | solution.py:10
  22.4 1.5 fusion.7
  23.9 12.3 %all-gather.1 = f32[512,128]{1,0:T(8,128)S(1)} all-gather(f32[128,128]{1,0:T(8,128)S(1)} %get-tuple-element.553), channel_id=3, replica_groups=mesh['wide'=64,'narrow'=4] {'narrow'}, dimensions={0}, use_global_device_ids=true | all-gather | bytes 327680 | tf_op jit(solution)/shard_map/all_gather | solution.py:10
  41.9 74.7 %all-gather.16.cloned.1.call-done = f32[192,32,128]{2,1,0:T(8,128)} async-done(((f32[3,32,128]{2,1,0:T(8,128)}), f32[192,32,128]{2,1,0:T(8,128)}) %all-gather.16.cloned.1.call-update) | async-done | bytes 3145744 | tf_op jit(solution)/shard_map/all_gather | solution.py:58
  117.4 1.5 collective-permute-start
  118.9 3.5 collective-permute-done
  122.6 4.7 collective-permute-done.1
  127.3 4.9 %collective-permute-done.2 = f32[32,128]{1,0:T(8,128)S(1)} collective-permute-done((f32[32,128]{1,0:T(8,128)S(1)}, f32[32,128]{1,0:T(8,128)S(1)}, u32[]{:S(2)}, u32[]{:S(2)}) %collective-permute-start.2) | collective-permute-done | bytes 16416 | tf_op jit(solution)/shard_map/ppermute | solution.py:63
  133.2 12.4 %all-gather.3 = f32[512,128]{1,0:T(8,128)S(1)} all-gather(f32[128,128]{1,0:T(8,128)S(1)} %fusion.15), channel_id=5, replica_groups=mesh['wide'=64,'narrow'=4] {'narrow'}, dimensions={0}, use_global_device_ids=true | all-gather | bytes 327680 | tf_op jit(solution)/shard_map/all_gather | solution.py:10
  145.6 12.2 %all-gather.4 = f32[512,128]{1,0:T(8,128)S(1)} all-gather(f32[128,128]{1,0:T(8,128)S(1)} %get-tuple-element.548), channel_id=6, replica_groups=mesh['wide'=64,'narrow'=4] {'narrow'}, dimensions={0}, use_global_device_ids=true | all-gather | bytes 327680 | tf_op jit(solution)/shard_map/all_gather | solution.py:10
  158.1 1.3 exponential_reduce_fusion.6
  160.3 74.3 %all-gather.18.cloned.1.call-done = f32[192,32,128]{2,1,0:T(8,128)} async-done(((f32[3,32,128]{2,1,0:T(8,128)}), f32[192,32,128]{2,1,0:T(8,128)}) %all-gather.18.cloned.1.call-update) | async-done | bytes 3145744 | tf_op jit(solution)/shard_map/all_gather | solution.py:58
  235.3 1.5 collective-permute-start.3
  236.8 3.5 collective-permute-done.3
  240.5 4.7 collective-permute-done.4
  245.2 4.9 %collective-permute-done.5 = f32[32,128]{1,0:T(8,128)S(1)} collective-permute-done((f32[32,128]{1,0:T(8,128)S(1)}, f32[32,128]{1,0:T(8,128)S(1)}, u32[]{:S(2)}, u32[]{:S(2)}) %collective-permute-start.5) | collective-permute-done | bytes 16416 | tf_op jit(solution)/shard_map/ppermute | solution.py:63
  251.1 12.4 %all-gather.6 = f32[512,128]{1,0:T(8,128)S(1)} all-gather(f32[128,128]{1,0:T(8,128)S(1)} %fusion.18), channel_id=8, replica_groups=mesh['wide'=64,'narrow'=4] {'narrow'}, dimensions={0}, use_global_device_ids=true | all-gather | bytes 327680 | tf_op jit(solution)/shard_map/all_gather | solution.py:10
  263.5 12.2 %all-gather.7 = f32[512,128]{1,0:T(8,128)S(1)} all-gather(f32[128,128]{1,0:T(8,128)S(1)} %get-tuple-element.543), channel_id=9, replica_groups=mesh['wide'=64,'narrow'=4] {'narrow'}, dimensions={0}, use_global_device_ids=true | all-gather | bytes 327680 | tf_op jit(solution)/shard_map/all_gather | solution.py:10
  278.7 73.7 %all-gather.20.cloned.1.call-done = f32[192,32,128]{2,1,0:T(8,128)} async-done(((f32[3,32,128]{2,1,0:T(8,128)}), f32[192,32,128]{2,1,0:T(8,128)}) %all-gather.20.cloned.1.call-update) | async-done | bytes 3145744 | tf_op jit(solution)/shard_map/all_gather | solution.py:58
  353.2 1.5 collective-permute-start.6
  354.7 3.5 collective-permute-done.6
  358.4 4.7 collective-permute-done.7
  364.4 3.7 collective-permute-done.8
  369.4 1.8 exponential_reduce_fusion.1
  373.8 7.7 %all-reduce.2 = (f32[4]{0:T(128)S(1)}, f32[4]{0:T(128)S(1)}) all-reduce(f32[4]{0:T(128)S(1)} %dynamic-update-slice, f32[4]{0:T(128)S(1)} %dynamic-update-slice.1), channel_id=1, replica_groups=mesh['wide'=64,'narrow'=4] {'narrow'}, use_global_device_ids=true, to_apply=%add | all-reduce | flops 8 | bytes 64
  381.6 9.7 %while.71 = (s32[]{:T(128)}, f32[]{:T(128)}, f32[]{:T(128)}, f32[4]{0:T(128)S(1)}, f32[4]{0:T(128)S(1)}, /*index=5*/s32[]{:T(128)}, s32[]{:T(128)}, s32[]{:T(128)}) while((s32[]{:T(128)}, f32[]{:T(128)}, f32[]{:T(128)}, f32[4]{0:T(128)S(1)}, f32[4]{0:T(128)S(1)}, /*index=5*/s32[]{:T(128)}, s32[]{:T(128)}, s32[]{:T(128)}) %tuple.163), condition=%wide.region_27.29_spmd, body=%wide.region_26.28_spmd.sunk | while | flops 11 | bytes 247 | solution.py:15
  392.4 36.8 %all-gather.14.cloned.1.call-done = f32[64,32,128]{2,1,0:T(8,128)} async-done(((f32[1,32,128]{2,1,0:T(8,128)}), f32[64,32,128]{2,1,0:T(8,128)}) %all-gather.14.cloned.1.call-update) | async-done | bytes 1048592 | tf_op jit(solution)/shard_map/all_gather | solution.py:86
  429.2 2.9 fusion.19
  432.1 21.6 %reduce-scatter.2.cloned.1.call-done = f32[32,128]{1,0:T(8,128)} async-done(((f32[128,128]{1,0:T(8,128)}), f32[32,128]{1,0:T(8,128)}) %reduce-scatter.2.cloned.1.call-update) | async-done | bytes 16400 | tf_op jit(solution)/shard_map/reduce_scatter | solution.py:78
  454.4 11.9 %all_gather.83 = f32[128,128]{1,0:T(8,128)S(1)} all-gather(f32[32,128]{1,0:T(8,128)S(1)} %sub.201), channel_id=1, replica_groups=mesh['wide'=64,'narrow'=4] {'narrow'}, dimensions={0}, use_global_device_ids=true | all-gather | bytes 81920 | tf_op jit(solution)/shard_map/all_gather | solution.py:91
  466.3 1.6 broadcast_subtract_fusion
  (85 shorter events, 22.1 us)
Async XLA Ops:
  7.2 15.2 %copy-start = (f32[1,32,128,128]{3,2,1,0:T(8,128)S(1)}, f32[1,32,128,128]{3,2,1,0:T(8,128)}, u32[]{:S(2)}) copy-start(f32[1,32,128,128]{3,2,1,0:T(8,128)} %param.15) | copy-start | bytes 6291460
  7.2 109.5 %all-gather.16.cloned.1.call-start = ((), (), s32[]{:S(2)}) async-start(), calls=%async_computation.3 | async-start | bytes 3194880 | tf_op jit(solution)/shard_map/all_gather | solution.py:58
  23.9 13.3 %copy-start.1 = (s32[64]{0:T(128)S(1)}, s32[64]{0:T(128)}, u32[]{:S(2)}) copy-start(s32[64]{0:T(128)} %param.16) | copy-start | bytes 772
  23.9 15.2 %copy-start.2 = (s32[64]{0:T(128)S(1)}, s32[64]{0:T(128)}, u32[]{:S(2)}) copy-start(s32[64]{0:T(128)} %param.17) | copy-start | bytes 772
  37.1 197.4 %all-gather.18.cloned.1.call-start = ((), (), s32[]{:S(2)}) async-start(), calls=%async_computation.4 | async-start | bytes 3194880 | tf_op jit(solution)/shard_map/all_gather | solution.py:58
  117.4 4.9 %collective-permute-start = (f32[32,128]{1,0:T(8,128)S(1)}, f32[32,128]{1,0:T(8,128)S(1)}, u32[]{:S(2)}, u32[]{:S(2)}) collective-permute-start(f32[32,128]{1,0:T(8,128)S(1)} %dynamic-slice_bitcast_fusion.2), channel_id=1, source_target_pairs={{0,1},{1,2},{2,3},{3,0},{4,5},{5,6},{6,7},{7,4},{8,9},{9,10},{10,1... | collective-permute-start | bytes 49160 | tf_op jit(solution)/shard_map/ppermute | solution.py:63
  122.3 4.9 %collective-permute-start.1 = (f32[32,128]{1,0:T(8,128)S(1)}, f32[32,128]{1,0:T(8,128)S(1)}, u32[]{:S(2)}, u32[]{:S(2)}) collective-permute-start(f32[32,128]{1,0:T(8,128)S(1)} %collective-permute-done), channel_id=1, source_target_pairs={{0,1},{1,2},{2,3},{3,0},{4,5},{5,6},{6,7},{7,4},{8,9},{9,10},{10,1... | collective-permute-start | bytes 49160 | tf_op jit(solution)/shard_map/ppermute | solution.py:63
  127.3 4.9 %collective-permute-start.2 = (f32[32,128]{1,0:T(8,128)S(1)}, f32[32,128]{1,0:T(8,128)S(1)}, u32[]{:S(2)}, u32[]{:S(2)}) collective-permute-start(f32[32,128]{1,0:T(8,128)S(1)} %collective-permute-done.1), channel_id=1, source_target_pairs={{0,1},{1,2},{2,3},{3,0},{4,5},{5,6},{6,7},{7,4},{8,9},{9,10},{10,1... | collective-permute-start | bytes 49160 | tf_op jit(solution)/shard_map/ppermute | solution.py:63
  160.2 192.3 %all-gather.20.cloned.1.call-start = ((), (), s32[]{:S(2)}) async-start(), calls=%async_computation.5 | async-start | bytes 3194880 | tf_op jit(solution)/shard_map/all_gather | solution.py:58
  235.3 4.9 %collective-permute-start.3 = (f32[32,128]{1,0:T(8,128)S(1)}, f32[32,128]{1,0:T(8,128)S(1)}, u32[]{:S(2)}, u32[]{:S(2)}) collective-permute-start(f32[32,128]{1,0:T(8,128)S(1)} %dynamic-slice_bitcast_fusion.1), channel_id=1, source_target_pairs={{0,1},{1,2},{2,3},{3,0},{4,5},{5,6},{6,7},{7,4},{8,9},{9,10},{10,1... | collective-permute-start | bytes 49160 | tf_op jit(solution)/shard_map/ppermute | solution.py:63
  240.2 4.9 %collective-permute-start.4 = (f32[32,128]{1,0:T(8,128)S(1)}, f32[32,128]{1,0:T(8,128)S(1)}, u32[]{:S(2)}, u32[]{:S(2)}) collective-permute-start(f32[32,128]{1,0:T(8,128)S(1)} %collective-permute-done.3), channel_id=1, source_target_pairs={{0,1},{1,2},{2,3},{3,0},{4,5},{5,6},{6,7},{7,4},{8,9},{9,10},{10,1... | collective-permute-start | bytes 49160 | tf_op jit(solution)/shard_map/ppermute | solution.py:63
  245.2 4.9 %collective-permute-start.5 = (f32[32,128]{1,0:T(8,128)S(1)}, f32[32,128]{1,0:T(8,128)S(1)}, u32[]{:S(2)}, u32[]{:S(2)}) collective-permute-start(f32[32,128]{1,0:T(8,128)S(1)} %collective-permute-done.4), channel_id=1, source_target_pairs={{0,1},{1,2},{2,3},{3,0},{4,5},{5,6},{6,7},{7,4},{8,9},{9,10},{10,1... | collective-permute-start | bytes 49160 | tf_op jit(solution)/shard_map/ppermute | solution.py:63
  275.8 87.3 %copy-start.3 = (s32[64]{0:T(128)S(1)}, s32[64]{0:T(128)}, u32[]{:S(2)}) copy-start(s32[64]{0:T(128)} %param.18) | copy-start | bytes 772
  275.8 88.0 %copy-start.4 = (u32[256]{0:T(256)S(1)}, u32[256]{0:T(256)}, u32[]{:S(2)}) copy-start(u32[256]{0:T(256)} %constant.221) | copy-start | bytes 3076
  278.1 151.1 %all-gather.14.cloned.1.call-start = ((), (), s32[]{:S(2)}) async-start(), calls=%async_computation.2 | async-start | bytes 1064960 | tf_op jit(solution)/shard_map/all_gather | solution.py:86
  278.7 175.0 %reduce-scatter.2.cloned.1.call-start = ((), (), s32[]{:S(2)}) async-start(), calls=%async_computation.1 | async-start | bytes 81920 | tf_op jit(solution)/shard_map/reduce_scatter | solution.py:78
  353.2 4.9 %collective-permute-start.6 = (f32[32,128]{1,0:T(8,128)S(1)}, f32[32,128]{1,0:T(8,128)S(1)}, u32[]{:S(2)}, u32[]{:S(2)}) collective-permute-start(f32[32,128]{1,0:T(8,128)S(1)} %dynamic-slice_bitcast_fusion), channel_id=1, source_target_pairs={{0,1},{1,2},{2,3},{3,0},{4,5},{5,6},{6,7},{7,4},{8,9},{9,10},{10,1... | collective-permute-start | bytes 49160 | tf_op jit(solution)/shard_map/ppermute | solution.py:63
  358.1 5.0 %collective-permute-start.7 = (f32[32,128]{1,0:T(8,128)S(1)}, f32[32,128]{1,0:T(8,128)S(1)}, u32[]{:S(2)}, u32[]{:S(2)}) collective-permute-start(f32[32,128]{1,0:T(8,128)S(1)} %collective-permute-done.6), channel_id=1, source_target_pairs={{0,1},{1,2},{2,3},{3,0},{4,5},{5,6},{6,7},{7,4},{8,9},{9,10},{10,1... | collective-permute-start | bytes 49160 | tf_op jit(solution)/shard_map/ppermute | solution.py:63
  363.1 4.9 %collective-permute-start.8 = (f32[32,128]{1,0:T(8,128)S(1)}, f32[32,128]{1,0:T(8,128)S(1)}, u32[]{:S(2)}, u32[]{:S(2)}) collective-permute-start(f32[32,128]{1,0:T(8,128)S(1)} %collective-permute-done.7), channel_id=1, source_target_pairs={{0,1},{1,2},{2,3},{3,0},{4,5},{5,6},{6,7},{7,4},{8,9},{9,10},{10,1... | collective-permute-start | bytes 49160 | tf_op jit(solution)/shard_map/ppermute | solution.py:63
Sparse Core Ops, SparseCore 0:
  37.3 79.3 all-gather.15
  160.3 74.1 all-gather.17
  278.2 74.1 all-gather.19
  355.1 74.0 all-gather.13
  432.1 21.4 reduce-scatter.1
